TPU v7x, 256 devices: a whole 4x4x8 slice. The times are simulated.
256 devices in a mesh: blk: 64 (over x_lo, z, y), rep: 4 (over x_hi, core).
Axes of the slice: x: 4 (x_hi: 2, x_lo: 2; x = x_hi * 2 + x_lo), y: 4, z: 8, core: 2. Of those that a mesh axis runs over, the one named last changes fastest.
Arguments:
- features: bfloat16 [16384, 768], P(('blk', 'rep')), may hold values from -6 to 6
- start_block: float32 [16384, 128], P(('blk', 'rep')), may hold values from -6 to 6
Outputs:
- spectral_rows: float32 [16384, 128], P(('blk', 'rep'))
All inputs are finite; a program needn't handle non-finite values.
Results may differ from a plain program's by a relative error of at most 0.0021.
The roundings to bfloat16 on the way count: a program that leaves them out, or rounds other values in their place, can miss the bound.
Values may be sent and summed in bfloat16 or wider, within the bound.
A program may use at most 64 MiB of HBM per device.

v0:
```python
import jax
import jax.numpy as jnp
from jax import lax
from jax.sharding import PartitionSpec as P

ITERS = 2


kernel_width = 0.04


def normalized(features):
    values = features.astype(jnp.float32)
    factor = 1.0 / jnp.sqrt(jnp.sum(values * values, axis=1, keepdims=True) + 1e-06)
    return (values * factor).astype(jnp.bfloat16)


def kernel_tile(left_rows, left_ids, right_rows, right_ids):
    cosine = lax.dot_general(
        left_rows, right_rows, (((1,), (1,)), ((), ())), preferred_element_type=jnp.float32
    )
    affinity = jnp.exp((cosine - 1.0) / kernel_width)
    return jnp.where(left_ids[:, None] == right_ids[None, :], jnp.zeros_like(affinity), affinity)


def body(features, start_block):
    own_rows = features.shape[0]
    blk_count = lax.axis_size("blk")
    rep_count = lax.axis_size("rep")
    blk_index = lax.axis_index("blk")
    rep_index = lax.axis_index("rep")
    block_size = own_rows * rep_count
    unit_rows = normalized(features)
    block_unit = lax.all_gather(unit_rows, "rep", axis=0, tiled=True)
    block_ids = blk_index * block_size + jnp.arange(block_size, dtype=jnp.int32)

    def piece_tile(piece_rows):
        places = jnp.arange(piece_rows.shape[0], dtype=jnp.int32)
        piece_ids = (places // own_rows * rep_count + rep_index) * own_rows + places % own_rows
        return kernel_tile(block_unit, block_ids, piece_rows, piece_ids)

    partial_degrees = jnp.sum(
        piece_tile(lax.all_gather(unit_rows, "blk", axis=0, tiled=True)), axis=1
    )
    own_inverse = 1.0 / jnp.sqrt(
        lax.psum_scatter(partial_degrees, "rep", scatter_dimension=0, tiled=True)
    )
    vectors = start_block
    for sweep_index in range(ITERS):
        scaled = (own_inverse[:, None] * vectors).astype(jnp.bfloat16)
        affinity = piece_tile(lax.all_gather(unit_rows, "blk", axis=0, tiled=True)).astype(
            jnp.bfloat16
        )
        partial_product = jnp.dot(
            affinity,
            lax.all_gather(scaled, "blk", axis=0, tiled=True),
            preferred_element_type=jnp.float32,
        )
        own_product = lax.psum_scatter(partial_product, "rep", scatter_dimension=0, tiled=True)
        image = own_inverse[:, None] * own_product
        gram_part = jnp.dot(
            image.T, image, precision=lax.Precision.HIGHEST, preferred_element_type=jnp.float32
        )
        gram = lax.psum(gram_part, ("blk", "rep"))
        lower = jnp.linalg.cholesky(gram)
        vectors = jax.scipy.linalg.solve_triangular(lower, image.T, lower=True).T
    spread = vectors * jnp.sqrt(jnp.float32(own_rows * blk_count * rep_count))
    return spread / jnp.sqrt(jnp.mean(spread * spread, axis=1, keepdims=True) + 1e-06)


def solution(mesh):
    return jax.shard_map(
        body,
        mesh=mesh,
        in_specs=(P(("blk", "rep"), None), P(("blk", "rep"), None)),
        out_specs=P(("blk", "rep"), None),
        check_vma=False,
    )
```

profile of v0, /device:TPU:1, one launch (start us, length us, event | category | flops | bytes accessed | tf_op | source)
XLA Modules:
  0.0 1532.0 jit_solution(17053174430922798434)
XLA Ops:
  6.5 1.0 fusion.9
  7.6 1.6 fusion.10
  9.3 1.3 dynamic-slice
  11.2 10.9 all_gather.14
  22.1 257.6 %all-gather.4.cloned.1.call-done = bf16[4096,768]{1,0:T(8,128)(2,1)} async-done(((bf16[64,768]{1,0:T(8,128)(2,1)}), bf16[4096,768]{1,0:T(8,128)(2,1)}) %all-gather.4.cloned.1.call-update) | async-done | bytes 6291472 | tf_op jit(solution)/shard_map/all_gather | solution.py:43
  279.7 4.8 fusion.42
  284.5 48.3 %all-reduce = f32[256]{0:T(256)S(1)} all-reduce(f32[256]{0:T(256)S(1)} %get-tuple-element.6), channel_id=2, replica_groups=mesh['blk'=64,'rep'=4] {'rep'}, use_global_device_ids=true, to_apply=%region_2.3.clone | all-reduce | flops 256 | bytes 2048
  332.9 0.7 multiply_convert_fusion
  333.6 249.8 %all-gather.6.cloned.1.call-done = bf16[4096,128]{1,0:T(8,128)(2,1)} async-done(((bf16[64,128]{1,0:T(8,128)(2,1)}), bf16[4096,128]{1,0:T(8,128)(2,1)}) %all-gather.6.cloned.1.call-update) | async-done | bytes 1048592 | tf_op jit(solution)/shard_map/all_gather | solution.py:56
  583.5 2.6 fusion.7
  586.1 74.0 %reduce-scatter.3.cloned.1.call-done = f32[64,128]{1,0:T(8,128)} async-done(((f32[256,128]{1,0:T(8,128)}), f32[64,128]{1,0:T(8,128)}) %reduce-scatter.3.cloned.1.call-update) | async-done | bytes 32784 | tf_op jit(solution)/shard_map/reduce_scatter | solution.py:59
  660.1 1.8 fusion.29
  662.0 242.4 %all-reduce.4.cloned.1.call-done = f32[128,128]{0,1:T(8,128)} async-done(((f32[128,128]{0,1:T(8,128)}), f32[128,128]{0,1:T(8,128)}) %all-reduce.4.cloned.1.call-update) | async-done | bytes 65552 | tf_op jit(solution)/shard_map/psum | solution.py:64
  904.4 0.9 copy.8
  905.3 0.9 fusion.16
  906.2 11.7 cholesky.44
  917.9 0.6 compare_reduce_fusion.1
  918.6 0.7 fusion.11
  919.3 9.8 custom-call.6
  929.1 1.6 fusion.4
  930.7 247.9 %all-gather.8.cloned.1.call-done = bf16[4096,128]{1,0:T(8,128)(2,1)} async-done(((bf16[64,128]{1,0:T(8,128)(2,1)}), bf16[4096,128]{1,0:T(8,128)(2,1)}) %all-gather.8.cloned.1.call-update) | async-done | bytes 1048592 | tf_op jit(solution)/shard_map/all_gather | solution.py:56
  1178.6 2.6 fusion.5
  1181.5 73.8 %reduce-scatter.5.cloned.1.call-done = f32[64,128]{1,0:T(8,128)} async-done(((f32[256,128]{1,0:T(8,128)}), f32[64,128]{1,0:T(8,128)}) %reduce-scatter.5.cloned.1.call-update) | async-done | bytes 32784 | tf_op jit(solution)/shard_map/reduce_scatter | solution.py:59
  1255.3 1.8 fusion.26
  1257.1 241.5 %all-reduce.6.cloned.1.call-done = f32[128,128]{0,1:T(8,128)} async-done(((f32[128,128]{0,1:T(8,128)}), f32[128,128]{0,1:T(8,128)}) %all-reduce.6.cloned.1.call-update) | async-done | bytes 65552 | tf_op jit(solution)/shard_map/psum | solution.py:64
  1498.6 0.9 copy.10
  1499.6 0.9 fusion.14
  1500.4 11.7 cholesky.55
  1512.8 0.7 fusion.12
  1513.5 9.8 custom-call.7
  1523.3 1.1 multiply_reduce_fusion
  1524.4 0.7 divide_bitcast_fusion
  (24 shorter events, 1.4 us)
Async XLA Ops:
  6.5 273.2 %all-gather.4.cloned.1.call-start = ((), (), s32[]{:S(2)}) async-start(), calls=%async_computation.2 | async-start | bytes 6389760 | tf_op jit(solution)/shard_map/all_gather | solution.py:43
  9.2 574.3 %all-gather.6.cloned.1.call-start = ((), (), s32[]{:S(2)}) async-start(), calls=%async_computation.3 | async-start | bytes 1064960 | tf_op jit(solution)/shard_map/all_gather | solution.py:56
  22.1 310.7 %copy-start = (f32[64,128]{1,0:T(8,128)S(1)}, f32[64,128]{1,0:T(8,128)}, u32[]{:S(2)}) copy-start(f32[64,128]{1,0:T(8,128)} %param.6) | copy-start | bytes 98308
  333.6 326.5 %reduce-scatter.3.cloned.1.call-start = ((), (), s32[]{:S(2)}) async-start(), calls=%async_computation.4 | async-start | bytes 163840 | tf_op jit(solution)/shard_map/reduce_scatter | solution.py:59
  586.1 318.4 %all-reduce.4.cloned.1.call-start = ((), (), s32[]{:S(2)}) async-start(), calls=%async_computation.5 | async-start | bytes 131072 | tf_op jit(solution)/shard_map/psum | solution.py:64
  661.9 516.7 %all-gather.8.cloned.1.call-start = ((), (), s32[]{:S(2)}) async-start(), calls=%async_computation.6 | async-start | bytes 1064960 | tf_op jit(solution)/shard_map/all_gather | solution.py:56
  930.7 324.6 %reduce-scatter.5.cloned.1.call-start = ((), (), s32[]{:S(2)}) async-start(), calls=%async_computation.7 | async-start | bytes 163840 | tf_op jit(solution)/shard_map/reduce_scatter | solution.py:59
  1181.2 317.4 %all-reduce.6.cloned.1.call-start = ((), (), s32[]{:S(2)}) async-start(), calls=%async_computation.8 | async-start | bytes 131072 | tf_op jit(solution)/shard_map/psum | solution.py:64
Sparse Core Ops, SparseCore 0:
  9.3 270.3 all-gather.3
  333.7 249.6 all-gather.5
  586.2 73.8 reduce-scatter.2
  666.4 238.0 all-reduce.3
  930.8 247.7 all-gather.7
  1181.4 73.8 reduce-scatter.4
  1260.8 237.7 all-reduce.5
where the time goes:
time: 1530 us
  waiting for transfers between devices  1390 us (91%)
  blocking collectives  59.2 us (4%)
  other arithmetic  51.5 us (3%)
  matrix products  16.3 us (1%)
    all_gather x2, waiting for transfers between devices, body(): lax.all_gather(scaled, 'blk', axis=0, tiled=True)  498 us
    psum x2, waiting for transfers between devices, body(): gram = lax.psum(gram_part, ('blk', 'rep'))  484 us
    all_gather x1, waiting for transfers between devices, body(): lax.all_gather(unit_rows, 'blk', axis=0, tiled=True)  258 us
    reduce_scatter x2, waiting for transfers between devices, body(): lax.psum_scatter(partial_product, 'rep', scatter_dimension=0, tiled=True)  148 us
    unnamed x1, blocking collectives  48.3 us
  transfers between devices with their start and end apart: 7, of which 7 were waited for; matrix products, arithmetic and copies ran while one was open for 0% of the time, Pallas kernels for 0%

commit v1 on v0

v1 whole, which is shorter than its diff:
```python
import functools

import jax
import jax.numpy as jnp
from jax import lax
from jax.experimental import pallas as pl
from jax.experimental.pallas import tpu as pltpu
from jax.sharding import PartitionSpec as P

ITERS = 2
KERNEL_WIDTH = 0.04
LOG2E = 1.4426950408889634
MESH = pl.DeviceIdType.MESH

NX, NY, NZ, NC = 4, 4, 8, 2
GROUP = 16
OWN = 64
KV = 128
SLICE = KV // GROUP
CHUNK = 256
F32 = jnp.float32
HIGHEST = lax.Precision.HIGHEST


def spread_of(v, k, axis):
    return jnp.broadcast_to(v[k : k + 1, :] if axis == 0 else v[:, k : k + 1], v.shape)


def inverse_cholesky(rows):
    lane = lax.broadcasted_iota(jnp.int32, (8, KV), 1)
    sub = lax.broadcasted_iota(jnp.int32, (8, KV), 0)
    rows = list(rows)
    out = []
    for p in range(16):
        base = 8 * p
        own = (lane >= base) & (lane < base + 8)
        factors = {i: [spread_of(rows[i], base + k, 1) for k in range(8)] for i in range(p, 16)}
        cols = list(factors[p])
        panel = jnp.where(own, (lane - base == sub).astype(F32), rows[p])
        done = jnp.zeros((8, KV), F32)
        for k in range(8):
            pivot = spread_of(cols[k], k, 0)
            recip = 1.0 / pivot
            at = sub == k
            row = spread_of(panel, k, 0) * recip
            done = jnp.where(at, panel * lax.rsqrt(pivot), done)
            panel = jnp.where(at, row, panel - cols[k] * row)
            for j in range(k + 1, 8):
                entry = spread_of(cols[j], k, 0) * recip
                cols[j] = jnp.where(at, entry, cols[j] - cols[k] * entry)
        out.append(jnp.where(lane <= base + sub, done, 0.0))
        spreads = [spread_of(panel, k, 0) for k in range(8)]
        for i in range(p + 1, 16):
            acc = jnp.where(own, 0.0, rows[i])
            for k in range(8):
                acc = acc - factors[i][k] * spreads[k]
            rows[i] = acc
    return out


(UNIT_ROWS, UNIT_COLS, START, DEGREES, PRODUCT, IMAGE, GRAM_A, GRAM_B, GRAM_C) = range(9)
PER_ITER = 5
STAGES = 4 + ITERS * PER_ITER


def kernel(
    features, start, out,
    unit_rows, unit_cols, tile, start_cols, sums, sums_in, inv_cols, scaled, part, part_in,
    image_cols, gram_part, gram_a, gram_mine, gram_b, gram_c, linv, send, recv,
):
    blk, rep = lax.axis_index("blk"), lax.axis_index("rep")
    x, y, z, c = (rep // 2) * 2 + blk // 32, blk % 4, (blk // 4) % 8, rep % 2
    a, b = z * 2 + c, x * 4 + y

    def device(px, py, pz, pc):
        return ((px % 2) * 32 + pz * 4 + py, (px // 2) * 2 + pc)

    a_peers, b_peers = [], []
    for dz in range(NZ):
        for dc in range(NC):
            if dz or dc:
                pz, pc = (z + dz) % NZ, (c + dc) % NC
                a_peers.append((pz * 2 + pc, device(x, y, pz, pc)))
    for dx in range(NX):
        for dy in range(NY):
            if dx or dy:
                px, py = (x + dx) % NX, (y + dy) % NY
                b_peers.append((px * 4 + py, device(px, py, z, c)))

    barrier = pltpu.get_barrier_semaphore()
    for _, peer in a_peers + b_peers:
        pl.semaphore_signal(barrier, inc=1, device_id=peer, device_id_type=MESH)

    values = features[...].astype(F32)
    factor = 1.0 / jnp.sqrt(jnp.sum(values * values, axis=1, keepdims=True) + 1e-06)
    unit = (values * factor).astype(jnp.bfloat16)
    unit_rows[b] = unit
    unit_cols[a] = unit
    start_cols[a] = start[...]
    pl.semaphore_wait(barrier, len(a_peers) + len(b_peers))

    def copy(stage, src, dst, mine, peer_slot, peer):
        return pltpu.make_async_remote_copy(
            src_ref=src, dst_ref=dst.at[mine], send_sem=send.at[stage, peer_slot],
            recv_sem=recv.at[stage, mine], device_id=peer, device_id_type=MESH,
        )

    def arrive(stage, dst, slot):
        pltpu.make_async_copy(dst.at[slot], dst.at[slot], recv.at[stage, slot]).wait()

    sent = []

    def put(stage, src, dst, mine, peer_slot, peer):
        one = copy(stage, src, dst, mine, peer_slot, peer)
        one.start()
        sent.append(one)

    for slot, peer in b_peers:
        put(UNIT_ROWS, unit_rows.at[b], unit_rows, b, slot, peer)
    sibling = device(x, y, z, 1 - c)
    for dz in range(1, NZ):
        pz = (z + dz) % NZ
        put(UNIT_COLS, unit_cols.at[a], unit_cols, a, pz * 2 + c, device(x, y, pz, c))
    put(UNIT_COLS, unit_cols.at[a], unit_cols, a, z * 2 + 1 - c, sibling)
    for slot, peer in a_peers:
        put(START, start_cols.at[a], start_cols, a, slot, peer)
    for dz in range(1, NZ):
        slot = ((z + dz) % NZ) * 2 + c
        arrive(UNIT_COLS, unit_cols, slot)
        put(UNIT_COLS, unit_cols.at[slot], unit_cols, slot, slot + 1 - 2 * c, sibling)
    for dz in range(0, NZ):
        arrive(UNIT_COLS, unit_cols, ((z + dz) % NZ) * 2 + 1 - c)
    for slot, _ in b_peers:
        arrive(UNIT_ROWS, unit_rows, slot)

    scale = LOG2E / KERNEL_WIDTH
    col_id = lax.broadcasted_iota(jnp.int32, (1, GROUP * OWN), 1) - a * OWN
    col_id = jnp.where((col_id >= 0) & (col_id < OWN), col_id, -1)
    total = jnp.zeros((8, GROUP * OWN), F32)
    for step in range(GROUP * OWN // CHUNK):
        slots = CHUNK // OWN
        rows = unit_rows[step * slots : (step + 1) * slots].reshape(CHUNK, -1)
        cosine = lax.dot_general(
            rows, unit_cols[...].reshape(GROUP * OWN, -1), (((1,), (1,)), ((), ())), preferred_element_type=F32
        )
        row_id = lax.broadcasted_iota(jnp.int32, (CHUNK, 1), 0) + (step * CHUNK - b * OWN)
        row_id = jnp.where((row_id >= 0) & (row_id < OWN), row_id, -2)
        affinity = jnp.where(row_id == col_id, 0.0, jnp.exp2(cosine * scale - scale))
        tile[step * CHUNK : (step + 1) * CHUNK, :] = affinity.astype(jnp.bfloat16)
        total = total + jnp.sum(affinity.reshape(CHUNK // 8, 8, GROUP * OWN), axis=0)
    total = jnp.sum(total, axis=0, keepdims=True)
    for k in range(8):
        sums[k : k + 1, :] = total[:, k * KV : (k + 1) * KV]

    for slot, peer in a_peers:
        put(DEGREES, sums, sums_in, a, slot, peer)
    sums_in[a] = sums[...]
    for slot, _ in a_peers:
        arrive(DEGREES, sums_in, slot)
    inverse = 1.0 / jnp.sqrt(jnp.sum(sums_in[...], axis=0))
    turned = jnp.concatenate([inverse, jnp.zeros((KV - 8, KV), F32)], axis=0).T
    for slot, _ in a_peers:
        arrive(START, start_cols, slot)
    for k in range(8):
        wide = jnp.broadcast_to(turned[:, k : k + 1], (KV, KV))
        inv_cols[k * KV : (k + 1) * KV, :] = wide
        scaled[k * KV : (k + 1) * KV, :] = (
            wide * start_cols[2 * k : 2 * k + 2].reshape(KV, KV)
        ).astype(jnp.bfloat16)
    own_inverse = inv_cols[pl.ds(pl.multiple_of(a * OWN, OWN), OWN), :]

    for it in range(ITERS):
        first = 4 + it * PER_ITER - PRODUCT
        last = it == ITERS - 1
        for step in range(GROUP * OWN // CHUNK):
            product = jnp.dot(
                tile[step * CHUNK : (step + 1) * CHUNK, :], scaled[...], preferred_element_type=F32
            )
            slots = CHUNK // OWN
            part[it, step * slots : (step + 1) * slots] = product.reshape(slots, OWN, KV)
        for slot, peer in b_peers:
            put(first + PRODUCT, part.at[it, slot], part_in.at[it], b, slot, peer)
        part_in[it, b] = part[it, b]
        for slot, _ in b_peers:
            arrive(first + PRODUCT, part_in.at[it], slot)
        image = own_inverse * jnp.sum(part_in[it], axis=0)

        gram = lax.dot_general(
            image, image, (((0,), (0,)), ((), ())), precision=HIGHEST, preferred_element_type=F32
        )
        gram_part[it] = gram.reshape(GROUP, SLICE, KV)
        for slot, peer in b_peers:
            put(first + GRAM_A, gram_part.at[it, slot], gram_a.at[it], b, slot, peer)
        gram_a[it, b] = gram_part[it, b]
        if not last:
            image_cols[a] = image
            for slot, peer in a_peers:
                put(first + IMAGE, image_cols.at[a], image_cols, a, slot, peer)
        for slot, _ in b_peers:
            arrive(first + GRAM_A, gram_a.at[it], slot)
        gram_mine[it] = jnp.sum(gram_a[it], axis=0)
        for slot, peer in a_peers:
            put(first + GRAM_B, gram_mine.at[it], gram_b.at[it], a, slot, peer)
        gram_b[it, a] = gram_mine[it]
        for slot, _ in a_peers:
            arrive(first + GRAM_B, gram_b.at[it], slot)
        gram_c[it, b] = jnp.sum(gram_b[it], axis=0)
        for slot, peer in b_peers:
            put(first + GRAM_C, gram_c.at[it, b], gram_c.at[it], b, slot, peer)
        for slot, _ in b_peers:
            arrive(first + GRAM_C, gram_c.at[it], slot)

        for i, row in enumerate(inverse_cholesky([gram_c[it, i] for i in range(GROUP)])):
            linv[8 * i : 8 * i + 8, :] = row

        def basis(block):
            return lax.dot_general(
                block, linv[...], (((1,), (1,)), ((), ())), precision=HIGHEST, preferred_element_type=F32
            )

        if last:
            spread = basis(image) * jnp.sqrt(F32(NX * NY * NZ * NC * OWN))
            out[...] = spread / jnp.sqrt(jnp.mean(spread * spread, axis=1, keepdims=True) + 1e-06)
        else:
            for slot, _ in a_peers:
                arrive(first + IMAGE, image_cols, slot)
            for step in range(GROUP * OWN // CHUNK):
                slots = CHUNK // OWN
                rows = slice(step * CHUNK, (step + 1) * CHUNK)
                vectors = basis(image_cols[step * slots : (step + 1) * slots].reshape(CHUNK, KV))
                scaled[rows, :] = (inv_cols[rows, :] * vectors).astype(jnp.bfloat16)

    for one in sent:
        one.wait_send()


def body(features, start):
    own, depth = features.shape
    side = GROUP * OWN
    bf16 = jnp.bfloat16
    vmem = pl.BlockSpec(memory_space=pltpu.VMEM)
    return pl.pallas_call(
        kernel,
        out_shape=jax.ShapeDtypeStruct((own, KV), F32),
        in_specs=[vmem, vmem],
        out_specs=vmem,
        scratch_shapes=[
            pltpu.VMEM((GROUP, OWN, depth), bf16),
            pltpu.VMEM((GROUP, OWN, depth), bf16),
            pltpu.VMEM((side, side), bf16),
            pltpu.VMEM((GROUP, OWN, KV), F32),
            pltpu.VMEM((8, KV), F32),
            pltpu.VMEM((GROUP, 8, KV), F32),
            pltpu.VMEM((side, KV), F32),
            pltpu.VMEM((side, KV), bf16),
            pltpu.VMEM((ITERS, GROUP, OWN, KV), F32),
            pltpu.VMEM((ITERS, GROUP, OWN, KV), F32),
            pltpu.VMEM((GROUP, OWN, KV), F32),
            pltpu.VMEM((ITERS, GROUP, SLICE, KV), F32),
            pltpu.VMEM((ITERS, GROUP, SLICE, KV), F32),
            pltpu.VMEM((ITERS, SLICE, KV), F32),
            pltpu.VMEM((ITERS, GROUP, SLICE, KV), F32),
            pltpu.VMEM((ITERS, GROUP, SLICE, KV), F32),
            pltpu.VMEM((KV, KV), F32),
            pltpu.SemaphoreType.DMA((STAGES, GROUP)),
            pltpu.SemaphoreType.DMA((STAGES, GROUP)),
        ],
        compiler_params=pltpu.CompilerParams(
            collective_id=0, has_side_effects=True, vmem_limit_bytes=48 * 2**20
        ),
        name="subspace",
    )(features, start)


def solution(mesh):
    return jax.shard_map(
        body,
        mesh=mesh,
        in_specs=(P(("blk", "rep"), None), P(("blk", "rep"), None)),
        out_specs=P(("blk", "rep"), None),
        check_vma=False,
    )
```

time: 1530 us -> 115 us (0.08)
  waiting for transfers between devices: 1390 us -> 0 us
  Pallas kernels: 0 us -> 113 us
  blocking collectives: 59.2 us -> 0 us
  other arithmetic: 51.5 us -> 0 us
  matrix products: 16.3 us -> 0 us
    all_gather x3 -> x0, waiting for transfers between devices: 755 us -> none  [the longest x2 498 us: body(): lax.all_gather(scaled, 'blk', axis=0, tiled=True)]
    psum x2 -> x0, waiting for transfers between devices: 484 us -> none  [body(): gram = lax.psum(gram_part, ('blk', 'rep'))]
    reduce_scatter x2 -> x0, waiting for transfers between devices: 148 us -> none  [body(): lax.psum_scatter(partial_product, 'rep', scatter_dimension=0, tiled=True)]
    pallas_call x0 -> x1, Pallas kernels: none -> 113 us  [body(): pl.pallas_call(kernel, out_shape=jax.ShapeDtypeStruct((own, KV), F32), in...]
    unnamed x1 -> x0, blocking collectives: 48.3 us -> none
    another operation x10 -> x0, other arithmetic: 45.7 us -> none  [the longest x6 24.8 us: body(): lower = jnp.linalg.cholesky(gram)]
  transfers between devices with their start and end apart: 7 -> 0, of which waited for: 7 -> 0; matrix products, arithmetic and copies ran while one was open for 0% -> 0% of each run, Pallas kernels for 0% -> 0%
where the time goes in v1:
time: 115 us
  Pallas kernels  113 us (98%)
  local copies, waits for them, and re-layouts  2.27 us (2%)
    pallas_call x1, Pallas kernels, body(): pl.pallas_call(kernel, out_shape=jax.ShapeDtypeStruct((own, KV), F32), in...  113 us

profile of v1, /device:TPU:1, one launch (start us, length us, event | category | flops | bytes accessed | tf_op | source)
XLA Modules:
  0.0 115.1 jit_solution(1827802892204126247)
XLA Ops:
  0.0 0.0 copy-start
  0.0 0.9 copy-done
  0.9 0.0 copy-start.1
  0.9 0.8 copy-done.1
  1.7 112.8 %subspace.1 = f32[64,128]{1,0:T(8,128)S(1)} custom-call(bf16[64,768]{1,0:T(8,128)(2,1)S(1)} %copy-done, f32[64,128]{1,0:T(8,128)S(1)} %copy-done.1), custom_call_target="tpu_custom_call" | custom-call | tf_op jit(solution)/shard_map/subspace/pallas_call | solution.py:242
  114.5 0.6 copy.4
Async XLA Ops:
  0.0 0.9 copy-start
  0.9 0.8 copy-start.1

commit v2 on v1

v2 whole, which is shorter than its diff:
```python
import functools

import jax
import jax.numpy as jnp
from jax import lax
from jax.experimental import pallas as pl
from jax.experimental.pallas import tpu as pltpu
from jax.sharding import PartitionSpec as P

ITERS = 2
KERNEL_WIDTH = 0.04
LOG2E = 1.4426950408889634
MESH = pl.DeviceIdType.MESH

NX, NY, NZ, NC = 4, 4, 8, 2
GROUP = 16
OWN = 64
KV = 128
SLICE = KV // GROUP
CHUNK = 256
F32 = jnp.float32
HIGHEST = lax.Precision.HIGHEST


def spread_of(v, k, axis):
    return jnp.broadcast_to(v[k : k + 1, :] if axis == 0 else v[:, k : k + 1], v.shape)


def inverse_cholesky(rows):
    lane = lax.broadcasted_iota(jnp.int32, (8, KV), 1)
    sub = lax.broadcasted_iota(jnp.int32, (8, KV), 0)
    rows = list(rows)
    out = []
    for p in range(16):
        base = 8 * p
        own = (lane >= base) & (lane < base + 8)
        factors = {i: [spread_of(rows[i], base + k, 1) for k in range(8)] for i in range(p, 16)}
        cols = list(factors[p])
        panel = jnp.where(own, (lane - base == sub).astype(F32), rows[p])
        done = jnp.zeros((8, KV), F32)
        for k in range(8):
            pivot = spread_of(cols[k], k, 0)
            recip = 1.0 / pivot
            at = sub == k
            row = spread_of(panel, k, 0) * recip
            done = jnp.where(at, panel * lax.rsqrt(pivot), done)
            panel = jnp.where(at, row, panel - cols[k] * row)
            for j in range(k + 1, 8):
                entry = spread_of(cols[j], k, 0) * recip
                cols[j] = jnp.where(at, entry, cols[j] - cols[k] * entry)
        out.append(jnp.where(lane <= base + sub, done, 0.0))
        spreads = [spread_of(panel, k, 0) for k in range(8)]
        for i in range(p + 1, 16):
            acc = jnp.where(own, 0.0, rows[i])
            for k in range(8):
                acc = acc - factors[i][k] * spreads[k]
            rows[i] = acc
    return out


(UNIT_Z, UNIT_XY, UNIT_CORE, START, START_CORE, DEGREES) = range(6)
(PRODUCT, GRAM_A, GRAM_B, GRAM_C, IMAGE, IMAGE_CORE) = range(6)
STAGES = 6 + 6 * ITERS
HALF = OWN // 2


def kernel(
    features_hbm, start_hbm, out,
    features, unit_rows, unit_cols, tile, start_cols, sums, sums_in, inv_cols, scaled, part, part_in,
    image_cols, gram_part, gram_a, gram_mine, gram_b, gram_c, linv,
    load, send, recv, ring, first_hop, chunk,
):
    blk, rep = lax.axis_index("blk"), lax.axis_index("rep")
    x, y, z, c = (rep // 2) * 2 + blk // 32, blk % 4, (blk // 4) % 8, rep % 2
    a, b = c * NZ + z, x * NY + y

    def device(px, py, pz, pc):
        return ((px % 2) * 32 + pz * 4 + py, (px // 2) * 2 + pc)

    def shifted(dx, dy, dz, dc):
        return (x + dx) % NX, (y + dy) % NY, (z + dz) % NZ, (c + dc) % NC

    def at(dx=0, dy=0, dz=0, dc=0):
        return device(*shifted(dx, dy, dz, dc))

    far_first = (2, 1, 3)
    near_first = (1, 3, 2)
    sibling = at(dc=1)
    barrier = pltpu.get_barrier_semaphore()
    near = [at(dx=d) for d in near_first] + [at(dy=d) for d in near_first] + [at(dz=1), at(dz=NZ - 1), sibling]
    for peer in near:
        pl.semaphore_signal(barrier, inc=1, device_id=peer, device_id_type=MESH)
    load_features = pltpu.make_async_copy(features_hbm, features, load.at[0])
    load_features.start()
    load_start = pltpu.make_async_copy(start_hbm, start_cols.at[a], load.at[1])
    load_start.start()

    load_features.wait()
    values = features[...].astype(F32)
    factor = 1.0 / jnp.sqrt(jnp.sum(values * values, axis=1, keepdims=True) + 1e-06)
    unit = (values * factor).astype(jnp.bfloat16).reshape(2, HALF, -1)
    unit_rows[pl.ds(2 * b, 2)] = unit
    unit_cols[pl.ds(2 * a, 2)] = unit
    pl.semaphore_wait(barrier, len(near))

    def put(src, dst, stage, arrival, peer):
        pltpu.make_async_remote_copy(
            src_ref=src, dst_ref=dst, send_sem=send.at[stage], recv_sem=arrival,
            device_id=peer, device_id_type=MESH,
        ).start()

    def wait_for(ref, semaphore):
        pltpu.make_async_copy(ref, ref, semaphore).wait()

    def put_row_half(px, py, h, peer, arrival):
        half = unit_rows.at[2 * (px * NY + py) + h]
        put(half, half, UNIT_XY, arrival, peer)

    def put_col_half(pz, pc, h, peer, stage, arrival):
        half = unit_cols.at[2 * (pc * NZ + pz) + h]
        put(half, half, stage, arrival, peer)

    for h in range(2):
        put_col_half(z, c, h, at(dz=1), UNIT_Z, ring.at[0, 0, h])
        put_col_half(z, c, h, at(dz=NZ - 1), UNIT_Z, ring.at[1, 0, h])
        for d in near_first:
            if h == 0:
                put_row_half(x, y, 0, at(dx=d), first_hop.at[0, NX - d])
                put_row_half(x, y, 1, at(dy=d), first_hop.at[1, NY - d])
            else:
                put_row_half(x, y, 1, at(dx=d), chunk.at[NX - d])
                put_row_half(x, y, 0, at(dy=d), chunk.at[0])
    for h in range(2):
        put_col_half(z, c, h, sibling, UNIT_CORE, recv.at[UNIT_CORE])

    def ring_step(way, d, h):
        pz = (z - d) % NZ if way == 0 else (z + d) % NZ
        half = unit_cols.at[2 * (c * NZ + pz) + h]
        wait_for(half, ring.at[way, d - 1, h])
        if d < 3 or (d == 3 and h == way):
            put_col_half(pz, c, h, at(dz=1 if way == 0 else NZ - 1), UNIT_Z, ring.at[way, d, h])
        put_col_half(pz, c, h, sibling, UNIT_CORE, recv.at[UNIT_CORE])

    def plane_step(d):
        px = (x + d) % NX
        wait_for(unit_rows.at[2 * (px * NY + y)], first_hop.at[0, d])
        for e in near_first:
            put_row_half(px, y, 0, at(dy=e), chunk.at[d])
        py = (y + d) % NY
        wait_for(unit_rows.at[2 * (x * NY + py) + 1], first_hop.at[1, d])
        for e in near_first:
            put_row_half(x, py, 1, at(dx=e), chunk.at[NX - e])

    for h in range(2):
        for way in range(2):
            ring_step(way, 1, h)
    plane_step(1)
    plane_step(3)
    for h in range(2):
        for way in range(2):
            ring_step(way, 2, h)
    plane_step(2)
    for h in range(2):
        for way in range(2):
            ring_step(way, 3, h)
    for way in range(2):
        ring_step(way, 4, way)

    load_start.wait()
    along_z = (1, 7, 2, 6, 3, 5, 4)
    for d in along_z:
        put(start_cols.at[a], start_cols.at[a], START, recv.at[START], at(dz=d))

    wait_for(unit_cols.at[pl.ds(0, 2 * NZ)], recv.at[UNIT_CORE])
    scale = LOG2E / KERNEL_WIDTH
    side = GROUP * OWN
    col_id = lax.broadcasted_iota(jnp.int32, (1, side), 1) - a * OWN
    col_id = jnp.where((col_id >= 0) & (col_id < OWN), col_id, -1)
    total = jnp.zeros((8, side), F32)
    for d in (0,) + near_first:
        px = (x + d) % NX
        wait_for(unit_rows.at[pl.ds(0, 7 if d else 3)], chunk.at[d])
        rows = unit_rows[pl.ds(px * 2 * NY, 2 * NY)].reshape(CHUNK, -1)
        cosine = lax.dot_general(
            rows, unit_cols[...].reshape(side, -1), (((1,), (1,)), ((), ())), preferred_element_type=F32
        )
        if d == 0:
            row_id = lax.broadcasted_iota(jnp.int32, (CHUNK, 1), 0) - y * OWN
            row_id = jnp.where((row_id >= 0) & (row_id < OWN), row_id, -2)
            affinity = jnp.where(row_id == col_id, 0.0, jnp.exp2(cosine * scale - scale))
        else:
            affinity = jnp.exp2(cosine * scale - scale)
        tile[pl.ds(pl.multiple_of(px * CHUNK, CHUNK), CHUNK), :] = affinity.astype(jnp.bfloat16)
        total = total + jnp.sum(affinity.reshape(CHUNK // 8, 8, side), axis=0)
    total = jnp.sum(total, axis=0, keepdims=True)
    for k in range(8):
        sums[k : k + 1, :] = total[:, k * KV : (k + 1) * KV]

    a_peers = [at(dz=d, dc=e) for d in along_z for e in range(NC)] + [sibling]
    b_shifts = [(dx, dy) for dx in (2, 1, 3, 0) for dy in (2, 1, 3, 0) if dx or dy]
    for peer in a_peers:
        put(sums, sums_in.at[a], DEGREES, recv.at[DEGREES], peer)
    sums_in[a] = sums[...]
    wait_for(start_cols.at[pl.ds(0, NZ - 1)], recv.at[START])
    mine = pl.ds(c * NZ, NZ)
    put(start_cols.at[mine], start_cols.at[mine], START_CORE, recv.at[START_CORE], sibling)
    wait_for(sums_in.at[pl.ds(0, GROUP - 1)], recv.at[DEGREES])
    inverse = 1.0 / jnp.sqrt(jnp.sum(sums_in[...], axis=0))
    turned = jnp.concatenate([inverse, jnp.zeros((KV - 8, KV), F32)], axis=0).T
    wait_for(start_cols.at[pl.ds(0, NZ)], recv.at[START_CORE])
    for k in range(8):
        wide = jnp.broadcast_to(turned[:, k : k + 1], (KV, KV))
        inv_cols[k * KV : (k + 1) * KV, :] = wide
        scaled[k * KV : (k + 1) * KV, :] = (
            wide * start_cols[2 * k : 2 * k + 2].reshape(KV, KV)
        ).astype(jnp.bfloat16)
    own_inverse = inv_cols[pl.ds(pl.multiple_of(a * OWN, OWN), OWN), :]

    for it in range(ITERS):
        first = 6 + 6 * it
        last = it == ITERS - 1
        slots = CHUNK // OWN
        for dx in (2, 1, 3, 0):
            px = (x + dx) % NX
            product = jnp.dot(
                tile[pl.ds(pl.multiple_of(px * CHUNK, CHUNK), CHUNK), :], scaled[...], preferred_element_type=F32
            )
            part[it, pl.ds(px * slots, slots)] = product.reshape(slots, OWN, KV)
            for dy in (2, 1, 3, 0):
                if dx or dy:
                    py = (y + dy) % NY
                    put(
                        part.at[it, px * NY + py], part_in.at[it, b], first + PRODUCT,
                        recv.at[first + PRODUCT], at(dx=dx, dy=dy),
                    )
        part_in[it, b] = part[it, b]
        wait_for(part_in.at[it, pl.ds(0, GROUP - 1)], recv.at[first + PRODUCT])
        image = own_inverse * jnp.sum(part_in[it], axis=0)
        if not last:
            image_cols[a] = image
        gram = lax.dot_general(
            image, image, (((0,), (0,)), ((), ())), precision=HIGHEST, preferred_element_type=F32
        )
        gram_part[it] = gram.reshape(GROUP, SLICE, KV)
        for dx, dy in b_shifts:
            px, py, _, _ = shifted(dx, dy, 0, 0)
            put(
                gram_part.at[it, px * NY + py], gram_a.at[it, b], first + GRAM_A,
                recv.at[first + GRAM_A], at(dx=dx, dy=dy),
            )
        gram_a[it, b] = gram_part[it, b]
        wait_for(gram_a.at[it, pl.ds(0, GROUP - 1)], recv.at[first + GRAM_A])
        gram_mine[it] = jnp.sum(gram_a[it], axis=0)
        for peer in a_peers:
            put(gram_mine.at[it], gram_b.at[it, a], first + GRAM_B, recv.at[first + GRAM_B], peer)
        if not last:
            for d in along_z:
                put(image_cols.at[a], image_cols.at[a], first + IMAGE, recv.at[first + IMAGE], at(dz=d))
        gram_b[it, a] = gram_mine[it]
        wait_for(gram_b.at[it, pl.ds(0, GROUP - 1)], recv.at[first + GRAM_B])
        gram_c[it, b] = jnp.sum(gram_b[it], axis=0)
        for dx, dy in b_shifts:
            put(
                gram_c.at[it, b], gram_c.at[it, b], first + GRAM_C, recv.at[first + GRAM_C], at(dx=dx, dy=dy)
            )
        wait_for(gram_c.at[it, pl.ds(0, GROUP - 1)], recv.at[first + GRAM_C])
        if not last:
            wait_for(image_cols.at[pl.ds(0, NZ - 1)], recv.at[first + IMAGE])
            put(
                image_cols.at[mine], image_cols.at[mine], first + IMAGE_CORE, recv.at[first + IMAGE_CORE], sibling
            )

        for i, row in enumerate(inverse_cholesky([gram_c[it, i] for i in range(GROUP)])):
            linv[8 * i : 8 * i + 8, :] = row

        def basis(block):
            return lax.dot_general(
                block, linv[...], (((1,), (1,)), ((), ())), precision=HIGHEST, preferred_element_type=F32
            )

        if last:
            spread = basis(image) * jnp.sqrt(F32(NX * NY * NZ * NC * OWN))
            out[...] = spread / jnp.sqrt(jnp.mean(spread * spread, axis=1, keepdims=True) + 1e-06)
        else:
            wait_for(image_cols.at[pl.ds(0, NZ)], recv.at[first + IMAGE_CORE])
            for step in range(GROUP * OWN // CHUNK):
                rows = slice(step * CHUNK, (step + 1) * CHUNK)
                vectors = basis(image_cols[step * slots : (step + 1) * slots].reshape(CHUNK, KV))
                scaled[rows, :] = (inv_cols[rows, :] * vectors).astype(jnp.bfloat16)

    wait_for(unit_cols.at[pl.ds(0, 14)], send.at[UNIT_Z])
    wait_for(unit_cols.at[pl.ds(0, 16)], send.at[UNIT_CORE])
    wait_for(unit_rows.at[pl.ds(0, 30)], send.at[UNIT_XY])
    wait_for(start_cols.at[pl.ds(0, NZ - 1)], send.at[START])
    wait_for(start_cols.at[pl.ds(0, NZ)], send.at[START_CORE])
    wait_for(sums_in.at[pl.ds(0, GROUP - 1)], send.at[DEGREES])
    for it in range(ITERS):
        first = 6 + 6 * it
        wait_for(part.at[it, pl.ds(0, GROUP - 1)], send.at[first + PRODUCT])
        for stage in (GRAM_A, GRAM_B, GRAM_C):
            wait_for(gram_a.at[it, pl.ds(0, GROUP - 1)], send.at[first + stage])
        if it < ITERS - 1:
            wait_for(image_cols.at[pl.ds(0, NZ - 1)], send.at[first + IMAGE])
            wait_for(image_cols.at[pl.ds(0, NZ)], send.at[first + IMAGE_CORE])


def body(features, start):
    own, depth = features.shape
    side = GROUP * OWN
    bf16 = jnp.bfloat16
    hbm = pl.BlockSpec(memory_space=pl.ANY)
    dma = pltpu.SemaphoreType.DMA
    return pl.pallas_call(
        kernel,
        out_shape=jax.ShapeDtypeStruct((own, KV), F32),
        in_specs=[hbm, hbm],
        out_specs=pl.BlockSpec(memory_space=pltpu.VMEM),
        scratch_shapes=[
            pltpu.VMEM((own, depth), bf16),
            pltpu.VMEM((2 * GROUP, HALF, depth), bf16),
            pltpu.VMEM((2 * GROUP, HALF, depth), bf16),
            pltpu.VMEM((side, side), bf16),
            pltpu.VMEM((GROUP, OWN, KV), F32),
            pltpu.VMEM((8, KV), F32),
            pltpu.VMEM((GROUP, 8, KV), F32),
            pltpu.VMEM((side, KV), F32),
            pltpu.VMEM((side, KV), bf16),
            pltpu.VMEM((ITERS, GROUP, OWN, KV), F32),
            pltpu.VMEM((ITERS, GROUP, OWN, KV), F32),
            pltpu.VMEM((GROUP, OWN, KV), F32),
            pltpu.VMEM((ITERS, GROUP, SLICE, KV), F32),
            pltpu.VMEM((ITERS, GROUP, SLICE, KV), F32),
            pltpu.VMEM((ITERS, SLICE, KV), F32),
            pltpu.VMEM((ITERS, GROUP, SLICE, KV), F32),
            pltpu.VMEM((ITERS, GROUP, SLICE, KV), F32),
            pltpu.VMEM((KV, KV), F32),
            dma((2,)),
            dma((STAGES,)),
            dma((STAGES,)),
            dma((2, 4, 2)),
            dma((2, 4)),
            dma((4,)),
        ],
        compiler_params=pltpu.CompilerParams(
            collective_id=0, has_side_effects=True, vmem_limit_bytes=48 * 2**20
        ),
        name="subspace",
    )(features, start)


def solution(mesh):
    return jax.shard_map(
        body,
        mesh=mesh,
        in_specs=(P(("blk", "rep"), None), P(("blk", "rep"), None)),
        out_specs=P(("blk", "rep"), None),
        check_vma=False,
    )
```

time: 115 us -> 94.2 us (0.82)
  Pallas kernels: 113 us -> 91.8 us
    pallas_call x1, Pallas kernels: 113 us -> 91.8 us  [body(): pl.pallas_call(kernel, out_shape=jax.ShapeDtypeStruct((own, KV), F32), in...]
where the time goes in v2:
time: 94.2 us; the launch traced here: 94.1 us
  Pallas kernels  91.8 us (97%)
  local copies, waits for them, and re-layouts  2.27 us (2%)
    pallas_call x1, Pallas kernels, body(): pl.pallas_call(kernel, out_shape=jax.ShapeDtypeStruct((own, KV), F32), in...  91.8 us
    unnamed x5, local copies, waits for them, and re-layouts  2.27 us

profile of v2, /device:TPU:1, one launch (start us, length us, event | category | flops | bytes accessed | tf_op | source)
XLA Modules:
  0.0 94.1 jit_solution(12908630081059915126)
XLA Ops:
  0.0 0.0 copy-start
  0.0 0.9 copy-done
  0.9 0.0 copy-start.1
  0.9 0.8 copy-done.1
  1.7 91.8 %subspace.1 = f32[64,128]{1,0:T(8,128)S(1)} custom-call(bf16[64,768]{1,0:T(8,128)(2,1)S(1)} %copy-done, f32[64,128]{1,0:T(8,128)S(1)} %copy-done.1), custom_call_target="tpu_custom_call" | custom-call | tf_op jit(solution)/shard_map/subspace/pallas_call | solution.py:313
  93.5 0.6 copy.4
Async XLA Ops:
  0.0 0.9 copy-start
  0.9 0.8 copy-start.1

commit v3 on v2

--- a/solution.py
+++ b/solution.py
@@ -34,33 +34,34 @@
     for p in range(16):
         base = 8 * p
         own = (lane >= base) & (lane < base + 8)
-        factors = {i: [spread_of(rows[i], base + k, 1) for k in range(8)] for i in range(p, 16)}
-        cols = list(factors[p])
+        cols = [spread_of(rows[p], base + k, 1) for k in range(8)]
         panel = jnp.where(own, (lane - base == sub).astype(F32), rows[p])
         done = jnp.zeros((8, KV), F32)
+        scale = jnp.ones((8, KV), F32)
         for k in range(8):
             pivot = spread_of(cols[k], k, 0)
             recip = 1.0 / pivot
-            at = sub == k
-            row = spread_of(panel, k, 0) * recip
-            done = jnp.where(at, panel * lax.rsqrt(pivot), done)
-            panel = jnp.where(at, row, panel - cols[k] * row)
+            here = sub == k
+            others = jnp.where(here, 0.0, cols[k])
             for j in range(k + 1, 8):
-                entry = spread_of(cols[j], k, 0) * recip
-                cols[j] = jnp.where(at, entry, cols[j] - cols[k] * entry)
+                cols[j] = cols[j] - (others * spread_of(cols[j], k, 0)) * recip
+            done = jnp.where(here, panel * lax.rsqrt(pivot), done)
+            scale = jnp.where(here, recip, scale)
+            panel = panel - (others * spread_of(panel, k, 0)) * recip
+        panel = panel * scale
         out.append(jnp.where(lane <= base + sub, done, 0.0))
         spreads = [spread_of(panel, k, 0) for k in range(8)]
         for i in range(p + 1, 16):
             acc = jnp.where(own, 0.0, rows[i])
             for k in range(8):
-                acc = acc - factors[i][k] * spreads[k]
+                acc = acc - spread_of(rows[i], base + k, 1) * spreads[k]
             rows[i] = acc
     return out
 
 
-(UNIT_Z, UNIT_XY, UNIT_CORE, START, START_CORE, DEGREES) = range(6)
-(PRODUCT, GRAM_A, GRAM_B, GRAM_C, IMAGE, IMAGE_CORE) = range(6)
-STAGES = 6 + 6 * ITERS
+(UNIT_Z, UNIT_XY, UNIT_CORE, START_Z, START_CORE, DEGREES) = range(6)
+(PRODUCT, GRAM_A, GRAM_B, GRAM_C, IMAGE_Z, IMAGE_FAR, IMAGE_CORE) = range(7)
+STAGES = 6 + 7 * ITERS
 HALF = OWN // 2
 
 
@@ -68,7 +69,7 @@
     features_hbm, start_hbm, out,
     features, unit_rows, unit_cols, tile, start_cols, sums, sums_in, inv_cols, scaled, part, part_in,
     image_cols, gram_part, gram_a, gram_mine, gram_b, gram_c, linv,
-    load, send, recv, ring, first_hop, chunk,
+    load, send, recv, unit_ring, start_ring, image_ring, first_hop, chunk,
 ):
     blk, rep = lax.axis_index("blk"), lax.axis_index("rep")
     x, y, z, c = (rep // 2) * 2 + blk // 32, blk % 4, (blk // 4) % 8, rep % 2
@@ -87,8 +88,10 @@
     near_first = (1, 3, 2)
     sibling = at(dc=1)
     barrier = pltpu.get_barrier_semaphore()
-    near = [at(dx=d) for d in near_first] + [at(dy=d) for d in near_first] + [at(dz=1), at(dz=NZ - 1), sibling]
-    for peer in near:
+    way = 1 - 2 * c
+    following, preceding = at(dz=way + NZ), at(dz=NZ - way)
+    near = [at(dx=d) for d in near_first] + [at(dy=d) for d in near_first] + [sibling]
+    for peer in near + [preceding]:
         pl.semaphore_signal(barrier, inc=1, device_id=peer, device_id_type=MESH)
     load_features = pltpu.make_async_copy(features_hbm, features, load.at[0])
     load_features.start()
@@ -101,7 +104,7 @@
     unit = (values * factor).astype(jnp.bfloat16).reshape(2, HALF, -1)
     unit_rows[pl.ds(2 * b, 2)] = unit
     unit_cols[pl.ds(2 * a, 2)] = unit
-    pl.semaphore_wait(barrier, len(near))
+    pl.semaphore_wait(barrier, len(near) + 1)
 
     def put(src, dst, stage, arrival, peer):
         pltpu.make_async_remote_copy(
@@ -116,30 +119,25 @@
         half = unit_rows.at[2 * (px * NY + py) + h]
         put(half, half, UNIT_XY, arrival, peer)
 
-    def put_col_half(pz, pc, h, peer, stage, arrival):
-        half = unit_cols.at[2 * (pc * NZ + pz) + h]
-        put(half, half, stage, arrival, peer)
-
-    for h in range(2):
-        put_col_half(z, c, h, at(dz=1), UNIT_Z, ring.at[0, 0, h])
-        put_col_half(z, c, h, at(dz=NZ - 1), UNIT_Z, ring.at[1, 0, h])
-        for d in near_first:
-            if h == 0:
-                put_row_half(x, y, 0, at(dx=d), first_hop.at[0, NX - d])
-                put_row_half(x, y, 1, at(dy=d), first_hop.at[1, NY - d])
-            else:
-                put_row_half(x, y, 1, at(dx=d), chunk.at[NX - d])
-                put_row_half(x, y, 0, at(dy=d), chunk.at[0])
-    for h in range(2):
-        put_col_half(z, c, h, sibling, UNIT_CORE, recv.at[UNIT_CORE])
-
-    def ring_step(way, d, h):
-        pz = (z - d) % NZ if way == 0 else (z + d) % NZ
-        half = unit_cols.at[2 * (c * NZ + pz) + h]
-        wait_for(half, ring.at[way, d - 1, h])
-        if d < 3 or (d == 3 and h == way):
-            put_col_half(pz, c, h, at(dz=1 if way == 0 else NZ - 1), UNIT_Z, ring.at[way, d, h])
-        put_col_half(pz, c, h, sibling, UNIT_CORE, recv.at[UNIT_CORE])
+    def hand_on(array, slot, ring, d, other, stage_z, stage_core):
+        block = array.at[slot]
+        if d or other:
+            wait_for(block, ring.at[d, other])
+        if d < 3 or (d == 3 and not other):
+            put(block, block, stage_z, ring.at[d + 1, other], following)
+        if not (d or other):
+            put(block, block, stage_core, ring.at[0, 1], sibling)
+        elif d:
+            put(block, block, stage_core, recv.at[stage_core], sibling)
+
+    def unit_step(d, other):
+        slot = ((c + other) % NC) * NZ + (z - d * way) % NZ
+        for h in range(2):
+            hand_on(unit_cols, 2 * slot + h, unit_ring.at[h], d, other, UNIT_Z, UNIT_CORE)
+
+    def start_step(d, other):
+        slot = ((c + other) % NC) * NZ + (z - d * way) % NZ
+        hand_on(start_cols, slot, start_ring, d, other, START_Z, START_CORE)
 
     def plane_step(d):
         px = (x + d) % NX
@@ -151,27 +149,26 @@
         for e in near_first:
             put_row_half(x, py, 1, at(dx=e), chunk.at[NX - e])
 
-    for h in range(2):
-        for way in range(2):
-            ring_step(way, 1, h)
-    plane_step(1)
-    plane_step(3)
-    for h in range(2):
-        for way in range(2):
-            ring_step(way, 2, h)
-    plane_step(2)
-    for h in range(2):
-        for way in range(2):
-            ring_step(way, 3, h)
-    for way in range(2):
-        ring_step(way, 4, way)
-
+    unit_step(0, 0)
+    for d in near_first:
+        put_row_half(x, y, 0, at(dx=d), first_hop.at[0, NX - d])
+        put_row_half(x, y, 1, at(dy=d), first_hop.at[1, NY - d])
+    unit_step(0, 1)
     load_start.wait()
-    along_z = (1, 7, 2, 6, 3, 5, 4)
-    for d in along_z:
-        put(start_cols.at[a], start_cols.at[a], START, recv.at[START], at(dz=d))
-
-    wait_for(unit_cols.at[pl.ds(0, 2 * NZ)], recv.at[UNIT_CORE])
+    start_step(0, 0)
+    for d in near_first:
+        put_row_half(x, y, 1, at(dx=d), chunk.at[NX - d])
+        put_row_half(x, y, 0, at(dy=d), chunk.at[0])
+    for d in range(1, 4):
+        unit_step(d, 0)
+        plane_step((1, 3, 2)[d - 1])
+        unit_step(d, 1)
+        if d > 1:
+            start_step(d - 1, 0)
+        start_step(d - 1, 1)
+    unit_step(4, 0)
+
+    wait_for(unit_cols.at[pl.ds(0, 2 * (NZ - 1))], recv.at[UNIT_CORE])
     scale = LOG2E / KERNEL_WIDTH
     side = GROUP * OWN
     col_id = lax.broadcasted_iota(jnp.int32, (1, side), 1) - a * OWN
@@ -192,22 +189,24 @@
             affinity = jnp.exp2(cosine * scale - scale)
         tile[pl.ds(pl.multiple_of(px * CHUNK, CHUNK), CHUNK), :] = affinity.astype(jnp.bfloat16)
         total = total + jnp.sum(affinity.reshape(CHUNK // 8, 8, side), axis=0)
+        if d == 0:
+            start_step(3, 0)
+            start_step(3, 1)
     total = jnp.sum(total, axis=0, keepdims=True)
     for k in range(8):
         sums[k : k + 1, :] = total[:, k * KV : (k + 1) * KV]
 
+    along_z = (4, 5, 3, 6, 2, 7, 1)
     a_peers = [at(dz=d, dc=e) for d in along_z for e in range(NC)] + [sibling]
     b_shifts = [(dx, dy) for dx in (2, 1, 3, 0) for dy in (2, 1, 3, 0) if dx or dy]
     for peer in a_peers:
         put(sums, sums_in.at[a], DEGREES, recv.at[DEGREES], peer)
     sums_in[a] = sums[...]
-    wait_for(start_cols.at[pl.ds(0, NZ - 1)], recv.at[START])
-    mine = pl.ds(c * NZ, NZ)
-    put(start_cols.at[mine], start_cols.at[mine], START_CORE, recv.at[START_CORE], sibling)
+    start_step(4, 0)
     wait_for(sums_in.at[pl.ds(0, GROUP - 1)], recv.at[DEGREES])
     inverse = 1.0 / jnp.sqrt(jnp.sum(sums_in[...], axis=0))
     turned = jnp.concatenate([inverse, jnp.zeros((KV - 8, KV), F32)], axis=0).T
-    wait_for(start_cols.at[pl.ds(0, NZ)], recv.at[START_CORE])
+    wait_for(start_cols.at[pl.ds(0, NZ - 1)], recv.at[START_CORE])
     for k in range(8):
         wide = jnp.broadcast_to(turned[:, k : k + 1], (KV, KV))
         inv_cols[k * KV : (k + 1) * KV, :] = wide
@@ -216,8 +215,21 @@
         ).astype(jnp.bfloat16)
     own_inverse = inv_cols[pl.ds(pl.multiple_of(a * OWN, OWN), OWN), :]
 
+    def image_step(first, d):
+        blocks = {1: image_cols.at[c * NZ + (z - d) % NZ], NZ - 1: image_cols.at[c * NZ + (z + d) % NZ]}
+        for i, (ahead, block) in enumerate(blocks.items()):
+            if d:
+                wait_for(block, image_ring.at[i, d])
+            if d < 3:
+                put(block, block, first + IMAGE_Z, image_ring.at[i, d + 1], at(dz=ahead))
+            elif ahead == 1:
+                for e in range(NC):
+                    put(block, block, first + IMAGE_FAR, recv.at[first + IMAGE_FAR], at(dz=1, dc=e))
+            if d or not i:
+                put(block, block, first + IMAGE_CORE, recv.at[first + IMAGE_CORE], sibling)
+
     for it in range(ITERS):
-        first = 6 + 6 * it
+        first = 6 + 7 * it
         last = it == ITERS - 1
         slots = CHUNK // OWN
         for dx in (2, 1, 3, 0):
@@ -238,6 +250,7 @@
         image = own_inverse * jnp.sum(part_in[it], axis=0)
         if not last:
             image_cols[a] = image
+            image_step(first, 0)
         gram = lax.dot_general(
             image, image, (((0,), (0,)), ((), ())), precision=HIGHEST, preferred_element_type=F32
         )
@@ -254,8 +267,7 @@
         for peer in a_peers:
             put(gram_mine.at[it], gram_b.at[it, a], first + GRAM_B, recv.at[first + GRAM_B], peer)
         if not last:
-            for d in along_z:
-                put(image_cols.at[a], image_cols.at[a], first + IMAGE, recv.at[first + IMAGE], at(dz=d))
+            image_step(first, 1)
         gram_b[it, a] = gram_mine[it]
         wait_for(gram_b.at[it, pl.ds(0, GROUP - 1)], recv.at[first + GRAM_B])
         gram_c[it, b] = jnp.sum(gram_b[it], axis=0)
@@ -263,12 +275,11 @@
             put(
                 gram_c.at[it, b], gram_c.at[it, b], first + GRAM_C, recv.at[first + GRAM_C], at(dx=dx, dy=dy)
             )
+        if not last:
+            image_step(first, 2)
         wait_for(gram_c.at[it, pl.ds(0, GROUP - 1)], recv.at[first + GRAM_C])
         if not last:
-            wait_for(image_cols.at[pl.ds(0, NZ - 1)], recv.at[first + IMAGE])
-            put(
-                image_cols.at[mine], image_cols.at[mine], first + IMAGE_CORE, recv.at[first + IMAGE_CORE], sibling
-            )
+            image_step(first, 3)
 
         for i, row in enumerate(inverse_cholesky([gram_c[it, i] for i in range(GROUP)])):
             linv[8 * i : 8 * i + 8, :] = row
@@ -279,10 +290,12 @@
             )
 
         if last:
-            spread = basis(image) * jnp.sqrt(F32(NX * NY * NZ * NC * OWN))
-            out[...] = spread / jnp.sqrt(jnp.mean(spread * spread, axis=1, keepdims=True) + 1e-06)
+            vectors = basis(image)
+            spread = vectors * jnp.sqrt(F32(NX * NY * NZ * NC * OWN))
+            out[...] = vectors / jnp.sqrt(jnp.mean(spread * spread, axis=1, keepdims=True) + 1e-06)
         else:
-            wait_for(image_cols.at[pl.ds(0, NZ)], recv.at[first + IMAGE_CORE])
+            wait_for(image_cols.at[pl.ds(0, NZ - 1)], recv.at[first + IMAGE_CORE])
+            wait_for(image_cols.at[pl.ds(0, NC)], recv.at[first + IMAGE_FAR])
             for step in range(GROUP * OWN // CHUNK):
                 rows = slice(step * CHUNK, (step + 1) * CHUNK)
                 vectors = basis(image_cols[step * slots : (step + 1) * slots].reshape(CHUNK, KV))
@@ -290,18 +303,19 @@
 
     wait_for(unit_cols.at[pl.ds(0, 14)], send.at[UNIT_Z])
     wait_for(unit_cols.at[pl.ds(0, 16)], send.at[UNIT_CORE])
+    wait_for(start_cols.at[pl.ds(0, 7)], send.at[START_Z])
+    wait_for(start_cols.at[pl.ds(0, 8)], send.at[START_CORE])
     wait_for(unit_rows.at[pl.ds(0, 30)], send.at[UNIT_XY])
-    wait_for(start_cols.at[pl.ds(0, NZ - 1)], send.at[START])
-    wait_for(start_cols.at[pl.ds(0, NZ)], send.at[START_CORE])
     wait_for(sums_in.at[pl.ds(0, GROUP - 1)], send.at[DEGREES])
     for it in range(ITERS):
-        first = 6 + 6 * it
+        first = 6 + 7 * it
         wait_for(part.at[it, pl.ds(0, GROUP - 1)], send.at[first + PRODUCT])
         for stage in (GRAM_A, GRAM_B, GRAM_C):
             wait_for(gram_a.at[it, pl.ds(0, GROUP - 1)], send.at[first + stage])
         if it < ITERS - 1:
-            wait_for(image_cols.at[pl.ds(0, NZ - 1)], send.at[first + IMAGE])
-            wait_for(image_cols.at[pl.ds(0, NZ)], send.at[first + IMAGE_CORE])
+            wait_for(image_cols.at[pl.ds(0, 6)], send.at[first + IMAGE_Z])
+            wait_for(image_cols.at[pl.ds(0, 2)], send.at[first + IMAGE_FAR])
+            wait_for(image_cols.at[pl.ds(0, 7)], send.at[first + IMAGE_CORE])
 
 
 def body(features, start):
@@ -310,7 +324,7 @@
     bf16 = jnp.bfloat16
     hbm = pl.BlockSpec(memory_space=pl.ANY)
     dma = pltpu.SemaphoreType.DMA
-    return pl.pallas_call(
+    unscaled = pl.pallas_call(
         kernel,
         out_shape=jax.ShapeDtypeStruct((own, KV), F32),
         in_specs=[hbm, hbm],
@@ -337,15 +351,18 @@
             dma((2,)),
             dma((STAGES,)),
             dma((STAGES,)),
-            dma((2, 4, 2)),
+            dma((2, 5, 2)),
+            dma((5, 2)),
+            dma((2, 4)),
             dma((2, 4)),
             dma((4,)),
         ],
         compiler_params=pltpu.CompilerParams(
-            collective_id=0, has_side_effects=True, vmem_limit_bytes=48 * 2**20
+            collective_id=0, has_side_effects=True, vmem_limit_bytes=55200 * 1024
         ),
         name="subspace",
     )(features, start)
+    return unscaled * jnp.sqrt(F32(NX * NY * NZ * NC * OWN))
 
 
 def solution(mesh):

time: 94.2 us -> 88.5 us (0.939)
  Pallas kernels: 91.8 us -> 87.7 us
  local copies, waits for them, and re-layouts: 2.27 us -> 0 us
    pallas_call x1, Pallas kernels: 91.8 us -> 87.7 us  [body(): pl.pallas_call(kernel, out_shape=jax.ShapeDtypeStruct((own, KV), F32), in...]
    unnamed x5 -> x0, local copies, waits for them, and re-layouts: 2.27 us -> none
where the time goes in v3:
time: 88.5 us; the launch traced here: 88.4 us
  Pallas kernels  87.7 us (99%)
    pallas_call x1, Pallas kernels, body(): pl.pallas_call(kernel, out_shape=jax.ShapeDtypeStruct((own, KV), F32), in...  87.7 us

profile of v3, /device:TPU:1, one launch (start us, length us, event | category | flops | bytes accessed | tf_op | source)
XLA Modules:
  0.0 88.4 jit_solution(5393212561487724007)
XLA Ops:
  0.0 87.7 %subspace.1 = f32[64,128]{1,0:T(8,128)S(1)} custom-call(bf16[64,768]{1,0:T(8,128)(2,1)} %features_hbm.1, f32[64,128]{1,0:T(8,128)} %start_hbm.1), custom_call_target="tpu_custom_call" | custom-call | tf_op jit(solution)/shard_map/subspace/pallas_call | solution.py:327
  87.8 0.6 broadcast_multiply_fusion

commit v4 on v3

--- a/solution.py
+++ b/solution.py
@@ -59,15 +59,17 @@
     return out
 
 
-(UNIT_Z, UNIT_XY, UNIT_CORE, START_Z, START_CORE, DEGREES) = range(6)
+(UNIT_XY, UNIT_Z, UNIT_FAR, UNIT_CORE, UNIT_CORE_FAR, START_Z, START_FAR, START_CORE, DEGREES) = range(9)
 (PRODUCT, GRAM_A, GRAM_B, GRAM_C, IMAGE_Z, IMAGE_FAR, IMAGE_CORE) = range(7)
-STAGES = 6 + 7 * ITERS
+STAGES = 9 + 7 * ITERS
+COL_ORDER = (0, 1, 7, 2, 6, 3, 5, 4)
+NEAR_COLS = 5 * NC * OWN
 HALF = OWN // 2
 
 
 def kernel(
     features_hbm, start_hbm, out,
-    features, unit_rows, unit_cols, tile, start_cols, sums, sums_in, inv_cols, scaled, part, part_in,
+    features, unit_rows, unit_cols, tile, start_cols, sums, sums_in, inverses, inv_cols, scaled, part, part_in,
     image_cols, gram_part, gram_a, gram_mine, gram_b, gram_c, linv,
     load, send, recv, unit_ring, start_ring, image_ring, first_hop, chunk,
 ):
@@ -90,12 +92,13 @@
     barrier = pltpu.get_barrier_semaphore()
     way = 1 - 2 * c
     following, preceding = at(dz=way + NZ), at(dz=NZ - way)
-    near = [at(dx=d) for d in near_first] + [at(dy=d) for d in near_first] + [sibling]
+    crossing = at(dz=way + NZ, dc=1)
+    near = [at(dx=d) for d in near_first] + [at(dy=d) for d in near_first] + [sibling, crossing]
     for peer in near + [preceding]:
         pl.semaphore_signal(barrier, inc=1, device_id=peer, device_id_type=MESH)
     load_features = pltpu.make_async_copy(features_hbm, features, load.at[0])
     load_features.start()
-    load_start = pltpu.make_async_copy(start_hbm, start_cols.at[a], load.at[1])
+    load_start = pltpu.make_async_copy(start_hbm, start_cols.at[c], load.at[1])
     load_start.start()
 
     load_features.wait()
@@ -103,7 +106,7 @@
     factor = 1.0 / jnp.sqrt(jnp.sum(values * values, axis=1, keepdims=True) + 1e-06)
     unit = (values * factor).astype(jnp.bfloat16).reshape(2, HALF, -1)
     unit_rows[pl.ds(2 * b, 2)] = unit
-    unit_cols[pl.ds(2 * a, 2)] = unit
+    unit_cols[pl.ds(2 * c, 2)] = unit
     pl.semaphore_wait(barrier, len(near) + 1)
 
     def put(src, dst, stage, arrival, peer):
@@ -119,82 +122,103 @@
         half = unit_rows.at[2 * (px * NY + py) + h]
         put(half, half, UNIT_XY, arrival, peer)
 
-    def hand_on(array, slot, ring, d, other, stage_z, stage_core):
-        block = array.at[slot]
+    def slot_of(d, other):
+        return (2 * (2 * d - c) if d else 0) + (c + other) % NC
+
+    far_slot = 2 * (NZ - 1) + c
+
+    def hand_on(array, index, ring, d, other, stages, core_arrival):
+        stage_z, stage_far, stage_core = stages
+        block = array.at[index(slot_of(d, other))]
         if d or other:
             wait_for(block, ring.at[d, other])
-        if d < 3 or (d == 3 and not other):
-            put(block, block, stage_z, ring.at[d + 1, other], following)
+        if d < 3:
+            put(block, array.at[index(slot_of(d + 1, other))], stage_z, ring.at[d + 1, other], following)
+        elif not other:
+            for e in range(NC):
+                put(block, array.at[index(far_slot)], stage_far, recv.at[stage_far], at(dz=way + NZ, dc=e))
         if not (d or other):
             put(block, block, stage_core, ring.at[0, 1], sibling)
         elif d:
-            put(block, block, stage_core, recv.at[stage_core], sibling)
+            put(block, block, stage_core, recv.at[core_arrival], sibling)
 
     def unit_step(d, other):
-        slot = ((c + other) % NC) * NZ + (z - d * way) % NZ
         for h in range(2):
-            hand_on(unit_cols, 2 * slot + h, unit_ring.at[h], d, other, UNIT_Z, UNIT_CORE)
+            hand_on(
+                unit_cols, lambda slot: 2 * slot + h, unit_ring.at[h], d, other,
+                (UNIT_Z, UNIT_FAR, UNIT_CORE), UNIT_CORE if d < 3 else UNIT_CORE_FAR,
+            )
 
     def start_step(d, other):
-        slot = ((c + other) % NC) * NZ + (z - d * way) % NZ
-        hand_on(start_cols, slot, start_ring, d, other, START_Z, START_CORE)
+        hand_on(
+            start_cols, lambda slot: slot, start_ring, d, other, (START_Z, START_FAR, START_CORE), START_CORE
+        )
 
     def plane_step(d):
         px = (x + d) % NX
         wait_for(unit_rows.at[2 * (px * NY + y)], first_hop.at[0, d])
-        for e in near_first:
+        for e in far_first:
             put_row_half(px, y, 0, at(dy=e), chunk.at[d])
         py = (y + d) % NY
         wait_for(unit_rows.at[2 * (x * NY + py) + 1], first_hop.at[1, d])
-        for e in near_first:
+        for e in far_first:
             put_row_half(x, py, 1, at(dx=e), chunk.at[NX - e])
 
     unit_step(0, 0)
-    for d in near_first:
+    for d in far_first:
         put_row_half(x, y, 0, at(dx=d), first_hop.at[0, NX - d])
         put_row_half(x, y, 1, at(dy=d), first_hop.at[1, NY - d])
     unit_step(0, 1)
     load_start.wait()
     start_step(0, 0)
-    for d in near_first:
-        put_row_half(x, y, 1, at(dx=d), chunk.at[NX - d])
-        put_row_half(x, y, 0, at(dy=d), chunk.at[0])
     for d in range(1, 4):
         unit_step(d, 0)
+        if d == 1:
+            for e in far_first:
+                put_row_half(x, y, 1, at(dx=e), chunk.at[NX - e])
+                put_row_half(x, y, 0, at(dy=e), chunk.at[0])
         plane_step((1, 3, 2)[d - 1])
         unit_step(d, 1)
         if d > 1:
             start_step(d - 1, 0)
         start_step(d - 1, 1)
-    unit_step(4, 0)
-
-    wait_for(unit_cols.at[pl.ds(0, 2 * (NZ - 1))], recv.at[UNIT_CORE])
+
     scale = LOG2E / KERNEL_WIDTH
     side = GROUP * OWN
-    col_id = lax.broadcasted_iota(jnp.int32, (1, side), 1) - a * OWN
-    col_id = jnp.where((col_id >= 0) & (col_id < OWN), col_id, -1)
-    total = jnp.zeros((8, side), F32)
-    for d in (0,) + near_first:
+
+    def tile_part(d, low, high):
         px = (x + d) % NX
-        wait_for(unit_rows.at[pl.ds(0, 7 if d else 3)], chunk.at[d])
         rows = unit_rows[pl.ds(px * 2 * NY, 2 * NY)].reshape(CHUNK, -1)
-        cosine = lax.dot_general(
-            rows, unit_cols[...].reshape(side, -1), (((1,), (1,)), ((), ())), preferred_element_type=F32
-        )
-        if d == 0:
+        cols = unit_cols[low // HALF : high // HALF].reshape(high - low, -1)
+        cosine = lax.dot_general(rows, cols, (((1,), (1,)), ((), ())), preferred_element_type=F32)
+        affinity = jnp.exp2(cosine * scale - scale)
+        if not (d or low):
             row_id = lax.broadcasted_iota(jnp.int32, (CHUNK, 1), 0) - y * OWN
             row_id = jnp.where((row_id >= 0) & (row_id < OWN), row_id, -2)
-            affinity = jnp.where(row_id == col_id, 0.0, jnp.exp2(cosine * scale - scale))
-        else:
-            affinity = jnp.exp2(cosine * scale - scale)
-        tile[pl.ds(pl.multiple_of(px * CHUNK, CHUNK), CHUNK), :] = affinity.astype(jnp.bfloat16)
-        total = total + jnp.sum(affinity.reshape(CHUNK // 8, 8, side), axis=0)
-        if d == 0:
+            col_id = lax.broadcasted_iota(jnp.int32, (1, high), 1) - c * OWN
+            col_id = jnp.where((col_id >= 0) & (col_id < OWN), col_id, -1)
+            affinity = jnp.where(row_id == col_id, 0.0, affinity)
+        tile[pl.ds(pl.multiple_of(px * CHUNK, CHUNK), CHUNK), low:high] = affinity.astype(jnp.bfloat16)
+        return jnp.sum(affinity.reshape(CHUNK // 8, 8, high - low), axis=0)
+
+    def rows_arrived(d):
+        wait_for(unit_rows.at[pl.ds(0, 7 if d else 3)], chunk.at[d])
+
+    wait_for(unit_cols.at[pl.ds(0, 8)], recv.at[UNIT_CORE])
+    wait_for(unit_cols.at[pl.ds(0, 4)], recv.at[UNIT_CORE_FAR])
+    wait_for(unit_cols.at[pl.ds(0, 4)], recv.at[UNIT_FAR])
+    near_total = jnp.zeros((8, side), F32)
+    for d in (0, 1, 3, 2):
+        rows_arrived(d)
+        near_total = near_total + tile_part(d, 0, side)
+        if not d:
             start_step(3, 0)
             start_step(3, 1)
-    total = jnp.sum(total, axis=0, keepdims=True)
-    for k in range(8):
-        sums[k : k + 1, :] = total[:, k * KV : (k + 1) * KV]
+    for total, low in ((near_total, 0),):
+        total = jnp.sum(total, axis=0, keepdims=True)
+        for k in range(total.shape[1] // KV):
+            pz = (z + COL_ORDER[low // KV + k]) % NZ
+            sums[pl.ds(pz, 1), :] = total[:, k * KV : (k + 1) * KV]
 
     along_z = (4, 5, 3, 6, 2, 7, 1)
     a_peers = [at(dz=d, dc=e) for d in along_z for e in range(NC)] + [sibling]
@@ -202,34 +226,41 @@
     for peer in a_peers:
         put(sums, sums_in.at[a], DEGREES, recv.at[DEGREES], peer)
     sums_in[a] = sums[...]
-    start_step(4, 0)
     wait_for(sums_in.at[pl.ds(0, GROUP - 1)], recv.at[DEGREES])
-    inverse = 1.0 / jnp.sqrt(jnp.sum(sums_in[...], axis=0))
-    turned = jnp.concatenate([inverse, jnp.zeros((KV - 8, KV), F32)], axis=0).T
-    wait_for(start_cols.at[pl.ds(0, NZ - 1)], recv.at[START_CORE])
+    inverses[...] = 1.0 / jnp.sqrt(jnp.sum(sums_in[...], axis=0))
+    ordered = [inverses[pl.ds((z + r) % NZ, 1), :] for r in COL_ORDER]
+    turned = jnp.concatenate(ordered + [jnp.zeros((KV - 8, KV), F32)], axis=0).T
+    wait_for(start_cols.at[pl.ds(0, 6)], recv.at[START_CORE])
+    wait_for(start_cols.at[pl.ds(0, 2)], recv.at[START_FAR])
     for k in range(8):
         wide = jnp.broadcast_to(turned[:, k : k + 1], (KV, KV))
         inv_cols[k * KV : (k + 1) * KV, :] = wide
         scaled[k * KV : (k + 1) * KV, :] = (
             wide * start_cols[2 * k : 2 * k + 2].reshape(KV, KV)
         ).astype(jnp.bfloat16)
-    own_inverse = inv_cols[pl.ds(pl.multiple_of(a * OWN, OWN), OWN), :]
+    own_inverse = inv_cols[pl.ds(pl.multiple_of(c * OWN, OWN), OWN), :]
 
     def image_step(first, d):
-        blocks = {1: image_cols.at[c * NZ + (z - d) % NZ], NZ - 1: image_cols.at[c * NZ + (z + d) % NZ]}
-        for i, (ahead, block) in enumerate(blocks.items()):
+        for i, ahead in enumerate((1, NZ - 1)):
+            block = image_cols.at[(2 * (2 * d - i) if d else 0) + c]
             if d:
                 wait_for(block, image_ring.at[i, d])
             if d < 3:
-                put(block, block, first + IMAGE_Z, image_ring.at[i, d + 1], at(dz=ahead))
-            elif ahead == 1:
+                put(
+                    block, image_cols.at[2 * (2 * d + 2 - i) + c], first + IMAGE_Z, image_ring.at[i, d + 1],
+                    at(dz=ahead),
+                )
+            elif not i:
                 for e in range(NC):
-                    put(block, block, first + IMAGE_FAR, recv.at[first + IMAGE_FAR], at(dz=1, dc=e))
+                    put(
+                        block, image_cols.at[far_slot], first + IMAGE_FAR, recv.at[first + IMAGE_FAR],
+                        at(dz=1, dc=e),
+                    )
             if d or not i:
                 put(block, block, first + IMAGE_CORE, recv.at[first + IMAGE_CORE], sibling)
 
     for it in range(ITERS):
-        first = 6 + 7 * it
+        first = 9 + 7 * it
         last = it == ITERS - 1
         slots = CHUNK // OWN
         for dx in (2, 1, 3, 0):
@@ -249,7 +280,7 @@
         wait_for(part_in.at[it, pl.ds(0, GROUP - 1)], recv.at[first + PRODUCT])
         image = own_inverse * jnp.sum(part_in[it], axis=0)
         if not last:
-            image_cols[a] = image
+            image_cols[c] = image
             image_step(first, 0)
         gram = lax.dot_general(
             image, image, (((0,), (0,)), ((), ())), precision=HIGHEST, preferred_element_type=F32
@@ -262,12 +293,12 @@
                 recv.at[first + GRAM_A], at(dx=dx, dy=dy),
             )
         gram_a[it, b] = gram_part[it, b]
+        if not last:
+            image_step(first, 1)
         wait_for(gram_a.at[it, pl.ds(0, GROUP - 1)], recv.at[first + GRAM_A])
         gram_mine[it] = jnp.sum(gram_a[it], axis=0)
         for peer in a_peers:
             put(gram_mine.at[it], gram_b.at[it, a], first + GRAM_B, recv.at[first + GRAM_B], peer)
-        if not last:
-            image_step(first, 1)
         gram_b[it, a] = gram_mine[it]
         wait_for(gram_b.at[it, pl.ds(0, GROUP - 1)], recv.at[first + GRAM_B])
         gram_c[it, b] = jnp.sum(gram_b[it], axis=0)
@@ -277,10 +308,8 @@
             )
         if not last:
             image_step(first, 2)
+            image_step(first, 3)
         wait_for(gram_c.at[it, pl.ds(0, GROUP - 1)], recv.at[first + GRAM_C])
-        if not last:
-            image_step(first, 3)
-
         for i, row in enumerate(inverse_cholesky([gram_c[it, i] for i in range(GROUP)])):
             linv[8 * i : 8 * i + 8, :] = row
 
@@ -301,14 +330,16 @@
                 vectors = basis(image_cols[step * slots : (step + 1) * slots].reshape(CHUNK, KV))
                 scaled[rows, :] = (inv_cols[rows, :] * vectors).astype(jnp.bfloat16)
 
-    wait_for(unit_cols.at[pl.ds(0, 14)], send.at[UNIT_Z])
-    wait_for(unit_cols.at[pl.ds(0, 16)], send.at[UNIT_CORE])
-    wait_for(start_cols.at[pl.ds(0, 7)], send.at[START_Z])
-    wait_for(start_cols.at[pl.ds(0, 8)], send.at[START_CORE])
+    for array, halves, stages in (
+        (unit_cols, 2, (UNIT_Z, UNIT_FAR, UNIT_CORE)),
+        (start_cols, 1, (START_Z, START_FAR, START_CORE)),
+    ):
+        for stage, blocks in zip(stages, (6, 2, 7)):
+            wait_for(array.at[pl.ds(0, blocks * halves)], send.at[stage])
     wait_for(unit_rows.at[pl.ds(0, 30)], send.at[UNIT_XY])
     wait_for(sums_in.at[pl.ds(0, GROUP - 1)], send.at[DEGREES])
     for it in range(ITERS):
-        first = 6 + 7 * it
+        first = 9 + 7 * it
         wait_for(part.at[it, pl.ds(0, GROUP - 1)], send.at[first + PRODUCT])
         for stage in (GRAM_A, GRAM_B, GRAM_C):
             wait_for(gram_a.at[it, pl.ds(0, GROUP - 1)], send.at[first + stage])
@@ -337,6 +368,7 @@
             pltpu.VMEM((GROUP, OWN, KV), F32),
             pltpu.VMEM((8, KV), F32),
             pltpu.VMEM((GROUP, 8, KV), F32),
+            pltpu.VMEM((8, KV), F32),
             pltpu.VMEM((side, KV), F32),
             pltpu.VMEM((side, KV), bf16),
             pltpu.VMEM((ITERS, GROUP, OWN, KV), F32),
@@ -351,8 +383,8 @@
             dma((2,)),
             dma((STAGES,)),
             dma((STAGES,)),
-            dma((2, 5, 2)),
-            dma((5, 2)),
+            dma((2, 4, 2)),
+            dma((4, 2)),
             dma((2, 4)),
             dma((2, 4)),
             dma((4,)),

time: 88.5 us -> 87.1 us (0.984)
  Pallas kernels: 87.7 us -> 86.4 us
    pallas_call x1, Pallas kernels: 87.7 us -> 86.4 us  [body(): pl.pallas_call(kernel, out_shape=jax.ShapeDtypeStruct((own, KV), F32), in...]
where the time goes in v4:
time: 87.1 us; the launch traced here: 87 us
  Pallas kernels  86.4 us (99%)
    pallas_call x1, Pallas kernels, body(): pl.pallas_call(kernel, out_shape=jax.ShapeDtypeStruct((own, KV), F32), in...  86.4 us

profile of v4, /device:TPU:1, one launch (start us, length us, event | category | flops | bytes accessed | tf_op | source)
XLA Modules:
  0.0 87.0 jit_solution(11675272658649175344)
XLA Ops:
  0.0 86.4 %subspace.1 = f32[64,128]{1,0:T(8,128)S(1)} custom-call(bf16[64,768]{1,0:T(8,128)(2,1)} %features_hbm.1, f32[64,128]{1,0:T(8,128)} %start_hbm.1), custom_call_target="tpu_custom_call" | custom-call | tf_op jit(solution)/shard_map/subspace/pallas_call | solution.py:358
  86.4 0.6 broadcast_multiply_fusion

commit v5 on v4

--- a/solution.py
+++ b/solution.py
@@ -26,34 +26,43 @@
     return jnp.broadcast_to(v[k : k + 1, :] if axis == 0 else v[:, k : k + 1], v.shape)
 
 
+PANEL = 2
+
+
 def inverse_cholesky(rows):
     lane = lax.broadcasted_iota(jnp.int32, (8, KV), 1)
     sub = lax.broadcasted_iota(jnp.int32, (8, KV), 0)
     rows = list(rows)
+    width = 8 * PANEL
     out = []
-    for p in range(16):
-        base = 8 * p
-        own = (lane >= base) & (lane < base + 8)
-        cols = [spread_of(rows[p], base + k, 1) for k in range(8)]
-        panel = jnp.where(own, (lane - base == sub).astype(F32), rows[p])
-        done = jnp.zeros((8, KV), F32)
-        scale = jnp.ones((8, KV), F32)
-        for k in range(8):
-            pivot = spread_of(cols[k], k, 0)
+    for p in range(16 // PANEL):
+        base = width * p
+        own = (lane >= base) & (lane < base + width)
+        mine = range(p * PANEL, (p + 1) * PANEL)
+        cols = [[spread_of(rows[i], base + k, 1) for i in mine] for k in range(width)]
+        panel = [jnp.where(own, (lane - base == sub + 8 * t).astype(F32), rows[i]) for t, i in enumerate(mine)]
+        done = [jnp.zeros((8, KV), F32) for _ in mine]
+        scale = [jnp.ones((8, KV), F32) for _ in mine]
+        for k in range(width):
+            t, r = divmod(k, 8)
+            pivot = spread_of(cols[k][t], r, 0)
             recip = 1.0 / pivot
-            here = sub == k
-            others = jnp.where(here, 0.0, cols[k])
-            for j in range(k + 1, 8):
-                cols[j] = cols[j] - (others * spread_of(cols[j], k, 0)) * recip
-            done = jnp.where(here, panel * lax.rsqrt(pivot), done)
-            scale = jnp.where(here, recip, scale)
-            panel = panel - (others * spread_of(panel, k, 0)) * recip
-        panel = panel * scale
-        out.append(jnp.where(lane <= base + sub, done, 0.0))
-        spreads = [spread_of(panel, k, 0) for k in range(8)]
-        for i in range(p + 1, 16):
+            here = sub == r
+            others = [jnp.where(here, 0.0, v) if u == t else v for u, v in enumerate(cols[k])]
+            for j in range(k + 1, width):
+                entry = spread_of(cols[j][t], r, 0)
+                cols[j] = [v - (other * entry) * recip for v, other in zip(cols[j], others)]
+            done[t] = jnp.where(here, panel[t] * lax.rsqrt(pivot), done[t])
+            scale[t] = jnp.where(here, recip, scale[t])
+            row = spread_of(panel[t], r, 0)
+            panel = [v - (other * row) * recip for v, other in zip(panel, others)]
+        panel = [v * factor for v, factor in zip(panel, scale)]
+        for t in range(PANEL):
+            out.append(jnp.where(lane <= base + 8 * t + sub, done[t], 0.0))
+        spreads = [spread_of(panel[k // 8], k % 8, 0) for k in range(width)]
+        for i in range((p + 1) * PANEL, 16):
             acc = jnp.where(own, 0.0, rows[i])
-            for k in range(8):
+            for k in range(width):
                 acc = acc - spread_of(rows[i], base + k, 1) * spreads[k]
             rows[i] = acc
     return out
@@ -171,6 +180,7 @@
     unit_step(0, 1)
     load_start.wait()
     start_step(0, 0)
+    start_step(0, 1)
     for d in range(1, 4):
         unit_step(d, 0)
         if d == 1:
@@ -179,9 +189,9 @@
                 put_row_half(x, y, 0, at(dy=e), chunk.at[0])
         plane_step((1, 3, 2)[d - 1])
         unit_step(d, 1)
-        if d > 1:
-            start_step(d - 1, 0)
-        start_step(d - 1, 1)
+        if d < 3:
+            start_step(d, 0)
+            start_step(d, 1)
 
     scale = LOG2E / KERNEL_WIDTH
     side = GROUP * OWN
@@ -226,6 +236,25 @@
     for peer in a_peers:
         put(sums, sums_in.at[a], DEGREES, recv.at[DEGREES], peer)
     sums_in[a] = sums[...]
+    for array, pieces, stages in (
+        (unit_cols, 2, (UNIT_Z, UNIT_FAR, UNIT_CORE)),
+        (start_cols, 1, (START_Z, START_FAR, START_CORE)),
+    ):
+        for stage, blocks in zip(stages, (6, 2, 7)):
+            wait_for(array.at[pl.ds(0, blocks * pieces)], send.at[stage])
+    wait_for(unit_rows.at[pl.ds(0, 30)], send.at[UNIT_XY])
+    wait_for(sums_in.at[pl.ds(0, GROUP - 1)], send.at[DEGREES])
+
+    def drain_iteration(it):
+        first = 9 + 7 * it
+        wait_for(part.at[it, pl.ds(0, GROUP - 1)], send.at[first + PRODUCT])
+        for stage in (GRAM_A, GRAM_B, GRAM_C):
+            wait_for(gram_a.at[it, pl.ds(0, GROUP - 1)], send.at[first + stage])
+        if it < ITERS - 1:
+            wait_for(image_cols.at[pl.ds(0, 6)], send.at[first + IMAGE_Z])
+            wait_for(image_cols.at[pl.ds(0, 2)], send.at[first + IMAGE_FAR])
+            wait_for(image_cols.at[pl.ds(0, 7)], send.at[first + IMAGE_CORE])
+
     wait_for(sums_in.at[pl.ds(0, GROUP - 1)], recv.at[DEGREES])
     inverses[...] = 1.0 / jnp.sqrt(jnp.sum(sums_in[...], axis=0))
     ordered = [inverses[pl.ds((z + r) % NZ, 1), :] for r in COL_ORDER]
@@ -277,6 +306,8 @@
                         recv.at[first + PRODUCT], at(dx=dx, dy=dy),
                     )
         part_in[it, b] = part[it, b]
+        if it:
+            drain_iteration(it - 1)
         wait_for(part_in.at[it, pl.ds(0, GROUP - 1)], recv.at[first + PRODUCT])
         image = own_inverse * jnp.sum(part_in[it], axis=0)
         if not last:
@@ -330,23 +361,7 @@
                 vectors = basis(image_cols[step * slots : (step + 1) * slots].reshape(CHUNK, KV))
                 scaled[rows, :] = (inv_cols[rows, :] * vectors).astype(jnp.bfloat16)
 
-    for array, halves, stages in (
-        (unit_cols, 2, (UNIT_Z, UNIT_FAR, UNIT_CORE)),
-        (start_cols, 1, (START_Z, START_FAR, START_CORE)),
-    ):
-        for stage, blocks in zip(stages, (6, 2, 7)):
-            wait_for(array.at[pl.ds(0, blocks * halves)], send.at[stage])
-    wait_for(unit_rows.at[pl.ds(0, 30)], send.at[UNIT_XY])
-    wait_for(sums_in.at[pl.ds(0, GROUP - 1)], send.at[DEGREES])
-    for it in range(ITERS):
-        first = 9 + 7 * it
-        wait_for(part.at[it, pl.ds(0, GROUP - 1)], send.at[first + PRODUCT])
-        for stage in (GRAM_A, GRAM_B, GRAM_C):
-            wait_for(gram_a.at[it, pl.ds(0, GROUP - 1)], send.at[first + stage])
-        if it < ITERS - 1:
-            wait_for(image_cols.at[pl.ds(0, 6)], send.at[first + IMAGE_Z])
-            wait_for(image_cols.at[pl.ds(0, 2)], send.at[first + IMAGE_FAR])
-            wait_for(image_cols.at[pl.ds(0, 7)], send.at[first + IMAGE_CORE])
+    drain_iteration(ITERS - 1)
 
 
 def body(features, start):

time: 87.1 us -> 85.7 us (0.984)
  Pallas kernels: 86.4 us -> 85 us
    pallas_call x1, Pallas kernels: 86.4 us -> 85 us  [body(): pl.pallas_call(kernel, out_shape=jax.ShapeDtypeStruct((own, KV), F32), in...]
where the time goes in v5:
time: 85.7 us; the launch traced here: 85.6 us
  Pallas kernels  85 us (99%)
    pallas_call x1, Pallas kernels, body(): pl.pallas_call(kernel, out_shape=jax.ShapeDtypeStruct((own, KV), F32), in...  85 us

profile of v5, /device:TPU:1, one launch (start us, length us, event | category | flops | bytes accessed | tf_op | source)
XLA Modules:
  0.0 85.6 jit_solution(517662013302809159)
XLA Ops:
  0.0 85.0 %subspace.1 = f32[64,128]{1,0:T(8,128)S(1)} custom-call(bf16[64,768]{1,0:T(8,128)(2,1)} %features_hbm.1, f32[64,128]{1,0:T(8,128)} %start_hbm.1), custom_call_target="tpu_custom_call" | custom-call | tf_op jit(solution)/shard_map/subspace/pallas_call | solution.py:373
  85.0 0.6 broadcast_multiply_fusion

commit v6 on v5

--- a/solution.py
+++ b/solution.py
@@ -45,8 +45,17 @@
         scale = [jnp.ones((8, KV), F32) for _ in mine]
         for k in range(width):
             t, r = divmod(k, 8)
-            pivot = spread_of(cols[k][t], r, 0)
-            recip = 1.0 / pivot
+            if k % 4 == 0:
+                block = {
+                    (j, m): spread_of(cols[m][t], j % 8, 0) for m in range(k, k + 4) for j in range(m, k + 4)
+                }
+                recips = {}
+                for q in range(k, k + 4):
+                    recips[q] = 1.0 / block[q, q]
+                    for m in range(q + 1, k + 4):
+                        for j in range(m, k + 4):
+                            block[j, m] = block[j, m] - (block[j, q] * block[m, q]) * recips[q]
+            pivot, recip = block[k, k], recips[k]
             here = sub == r
             others = [jnp.where(here, 0.0, v) if u == t else v for u, v in enumerate(cols[k])]
             for j in range(k + 1, width):
@@ -74,6 +83,8 @@
 COL_ORDER = (0, 1, 7, 2, 6, 3, 5, 4)
 NEAR_COLS = 5 * NC * OWN
 HALF = OWN // 2
+PIECES = 4
+PIECE = OWN // PIECES
 
 
 def kernel(
@@ -113,9 +124,9 @@
     load_features.wait()
     values = features[...].astype(F32)
     factor = 1.0 / jnp.sqrt(jnp.sum(values * values, axis=1, keepdims=True) + 1e-06)
-    unit = (values * factor).astype(jnp.bfloat16).reshape(2, HALF, -1)
-    unit_rows[pl.ds(2 * b, 2)] = unit
-    unit_cols[pl.ds(2 * c, 2)] = unit
+    unit = (values * factor).astype(jnp.bfloat16)
+    unit_rows[pl.ds(2 * b, 2)] = unit.reshape(2, HALF, -1)
+    unit_cols[pl.ds(PIECES * c, PIECES)] = unit.reshape(PIECES, PIECE, -1)
     pl.semaphore_wait(barrier, len(near) + 1)
 
     def put(src, dst, stage, arrival, peer):
@@ -152,9 +163,9 @@
             put(block, block, stage_core, recv.at[core_arrival], sibling)
 
     def unit_step(d, other):
-        for h in range(2):
+        for h in range(PIECES):
             hand_on(
-                unit_cols, lambda slot: 2 * slot + h, unit_ring.at[h], d, other,
+                unit_cols, lambda slot: PIECES * slot + h, unit_ring.at[h], d, other,
                 (UNIT_Z, UNIT_FAR, UNIT_CORE), UNIT_CORE if d < 3 else UNIT_CORE_FAR,
             )
 
@@ -199,7 +210,7 @@
     def tile_part(d, low, high):
         px = (x + d) % NX
         rows = unit_rows[pl.ds(px * 2 * NY, 2 * NY)].reshape(CHUNK, -1)
-        cols = unit_cols[low // HALF : high // HALF].reshape(high - low, -1)
+        cols = unit_cols[low // PIECE : high // PIECE].reshape(high - low, -1)
         cosine = lax.dot_general(rows, cols, (((1,), (1,)), ((), ())), preferred_element_type=F32)
         affinity = jnp.exp2(cosine * scale - scale)
         if not (d or low):
@@ -214,9 +225,9 @@
     def rows_arrived(d):
         wait_for(unit_rows.at[pl.ds(0, 7 if d else 3)], chunk.at[d])
 
-    wait_for(unit_cols.at[pl.ds(0, 8)], recv.at[UNIT_CORE])
-    wait_for(unit_cols.at[pl.ds(0, 4)], recv.at[UNIT_CORE_FAR])
-    wait_for(unit_cols.at[pl.ds(0, 4)], recv.at[UNIT_FAR])
+    wait_for(unit_cols.at[pl.ds(0, 4 * PIECES)], recv.at[UNIT_CORE])
+    wait_for(unit_cols.at[pl.ds(0, 2 * PIECES)], recv.at[UNIT_CORE_FAR])
+    wait_for(unit_cols.at[pl.ds(0, 2 * PIECES)], recv.at[UNIT_FAR])
     near_total = jnp.zeros((8, side), F32)
     for d in (0, 1, 3, 2):
         rows_arrived(d)
@@ -237,7 +248,7 @@
         put(sums, sums_in.at[a], DEGREES, recv.at[DEGREES], peer)
     sums_in[a] = sums[...]
     for array, pieces, stages in (
-        (unit_cols, 2, (UNIT_Z, UNIT_FAR, UNIT_CORE)),
+        (unit_cols, PIECES, (UNIT_Z, UNIT_FAR, UNIT_CORE)),
         (start_cols, 1, (START_Z, START_FAR, START_CORE)),
     ):
         for stage, blocks in zip(stages, (6, 2, 7)):
@@ -378,7 +389,7 @@
         scratch_shapes=[
             pltpu.VMEM((own, depth), bf16),
             pltpu.VMEM((2 * GROUP, HALF, depth), bf16),
-            pltpu.VMEM((2 * GROUP, HALF, depth), bf16),
+            pltpu.VMEM((PIECES * GROUP, PIECE, depth), bf16),
             pltpu.VMEM((side, side), bf16),
             pltpu.VMEM((GROUP, OWN, KV), F32),
             pltpu.VMEM((8, KV), F32),
@@ -398,7 +409,7 @@
             dma((2,)),
             dma((STAGES,)),
             dma((STAGES,)),
-            dma((2, 4, 2)),
+            dma((PIECES, 4, 2)),
             dma((4, 2)),
             dma((2, 4)),
             dma((2, 4)),

time: 85.7 us -> 85.4 us (level)
  no operation moved by 1% of the time
where the time goes in v6:
time: 85.4 us; the launch traced here: 85.3 us
  Pallas kernels  84.6 us (99%)
    pallas_call x1, Pallas kernels, body(): pl.pallas_call(kernel, out_shape=jax.ShapeDtypeStruct((own, KV), F32), in...  84.6 us

profile of v6, /device:TPU:1, one launch (start us, length us, event | category | flops | bytes accessed | tf_op | source)
XLA Modules:
  0.0 85.3 jit_solution(3040182502633761414)
XLA Ops:
  0.0 84.6 %subspace.1 = f32[64,128]{1,0:T(8,128)S(1)} custom-call(bf16[64,768]{1,0:T(8,128)(2,1)} %features_hbm.1, f32[64,128]{1,0:T(8,128)} %start_hbm.1), custom_call_target="tpu_custom_call" | custom-call | tf_op jit(solution)/shard_map/subspace/pallas_call | solution.py:384
  84.6 0.6 broadcast_multiply_fusion
